TPU v7x, 32 devices: a whole 2x2x4 slice. The times are simulated.
32 devices in a mesh: groups: 2 (over y), grid: 4 (over z), layer: 4 (over x, core).
Axes of the slice: x: 2, y: 2, z: 4, core: 2. Of those that a mesh axis runs over, the one named last changes fastest.
Arguments:
- blocks: bfloat16 [64, 4, 128, 128], P(('groups', 'grid', 'layer')), parts along dimension 0, may hold values from -5 to 5
- columns: int32 [64, 4], P('groups'), parts along dimension 0, may hold values from 0 to 31, as said below
Outputs:
- sign_iterate: bfloat16 [64, 4, 128, 128], P(('groups', 'grid', 'layer')), parts along dimension 0
There are 2 independent parts, one for each index of `groups`. A program takes and returns all parts, laid end to end along the dimension named above; each array names one. Nothing has to cross between parts.
Inputs may be any that keep to these rules, and one draw needn't show every extreme that they name: Slot 0 of block row i holds i. The other kept columns of a row are distinct block rows of panels whose grid index differs from the row's by exactly 1 cyclically, never rows of the same device; panel h holds block rows h * 8 to (h + 1) * 8 - 1. For each device and each of the 2 signed distances, at most 4 kept columns of its block rows lie at that distance, and exactly 4 for some device and distance.
All inputs are finite; a program needn't handle non-finite values.
Results may differ from a plain program's by a relative error of at most 0.0056.
Values may be sent and summed in bfloat16 or wider, within the bound.
A program may use at most 64 MiB of HBM per device.

v0:
```python
import jax
import jax.numpy as jnp
from jax import lax
from jax.sharding import PartitionSpec as P

STEPS = 2


def from_behind(block, axis, distance):
    devices = range(lax.axis_size(axis))
    route = [((i - distance) % len(devices), i) for i in devices]
    return lax.ppermute(block, axis, route)


def pattern_product(multiplier, operand, context):
    (
        own_cols,
        own_global,
        send_list,
        send_valid,
        columns,
        grid_pos,
        grid_size,
        panel_len,
        distances,
    ) = context
    rows_own = multiplier.shape[0]
    slots = multiplier.shape[1]
    width = multiplier.shape[2]
    flat_list = send_list.reshape(-1)
    flat_valid = send_valid.reshape(-1)
    piece = lax.all_gather(operand, "layer", axis=0, tiled=True)
    picker = (
        (flat_list[:, None] == jnp.arange(piece.shape[0])[None, :]) & flat_valid[:, None]
    ).astype(jnp.bfloat16)
    chosen = jnp.einsum("rn,nuij->ruij", picker, piece, preferred_element_type=jnp.float32)
    packed = chosen.astype(jnp.bfloat16)
    packed = packed.reshape(send_list.shape + (slots, width, width))
    arrived = []
    for kind in range(len(distances)):
        arrived.append(from_behind((packed[kind], send_list[kind]), "grid", -distances[kind]))
    cand_blocks = jnp.concatenate([operand] + [entry[0] for entry in arrived], axis=0)
    cand_parts = [own_global]
    for kind in range(len(distances)):
        source = (grid_pos + distances[kind]) % grid_size
        cand_parts.append(source * panel_len + arrived[kind][1])
    cand_rows = jnp.concatenate(cand_parts, axis=0).astype(jnp.int32)
    cand_cols = jnp.take(columns, cand_rows, axis=0)
    wanted = own_cols.reshape(-1)
    matches = wanted[:, None] == cand_rows[None, :]
    gathered = jnp.einsum(
        "ac,cuij->auij",
        matches.astype(jnp.bfloat16),
        cand_blocks,
        preferred_element_type=jnp.float32,
    ).astype(jnp.bfloat16)
    gathered_cols = jnp.max(jnp.where(matches[:, :, None], cand_cols[None, :, :], -1), axis=1)
    partial_value = jnp.einsum(
        "aij,aujk->auik",
        multiplier.reshape(-1, width, width),
        gathered,
        preferred_element_type=jnp.float32,
    )
    agree = (
        gathered_cols.reshape(rows_own, slots, slots)[:, :, :, None] == own_cols[:, None, None, :]
    ).astype(jnp.float32)
    summed = jnp.einsum(
        "qtus,qtuik->qsik",
        agree,
        partial_value.reshape(rows_own, slots, slots, width, width),
        precision=lax.Precision.HIGHEST,
    )
    return summed * (2.0 * width) ** (-0.5)


def local(blocks, columns):
    rows_own = blocks.shape[0]
    slots = blocks.shape[1]
    grid_size = lax.axis_size("grid")
    layer_size = lax.axis_size("layer")
    panel_len = rows_own * layer_size
    grid_pos = lax.axis_index("grid")
    layer_pos = lax.axis_index("layer")
    first_row = (grid_pos * layer_size + layer_pos) * rows_own
    own_global = first_row + jnp.arange(rows_own)
    own_cols = lax.dynamic_slice_in_dim(columns, first_row, rows_own, 0)
    reach = min(3, (grid_size - 1) // 2)
    moved_slots = rows_own * (slots - 1)
    pack_len = 2 * ((moved_slots + 4 * reach - 1) // (4 * reach))
    distances = [offset + 1 for offset in range(reach)] + [-(offset + 1) for offset in range(reach)]
    slot_index = jnp.arange(moved_slots, dtype=jnp.int32)
    position = jnp.arange(pack_len, dtype=jnp.int32)
    list_parts = []
    valid_parts = []
    for shift_by in distances:
        source_grid = (grid_pos - shift_by) % grid_size
        source_start = (source_grid * layer_size + layer_pos) * rows_own
        source_cols = lax.dynamic_slice_in_dim(columns, source_start, rows_own, 0)[:, 1:].reshape(
            -1
        )
        matched = source_cols // panel_len == grid_pos
        ordering = jnp.argsort(jnp.where(matched, 0, moved_slots) + slot_index)[:pack_len]
        local_rows = source_cols[ordering] - grid_pos * panel_len
        counted = jnp.sum(matched.astype(jnp.int32))
        valid_now = position < counted
        list_parts.append(jnp.where(valid_now, local_rows, 0))
        valid_parts.append(valid_now)
    send_list = jnp.stack(list_parts, axis=0)
    send_valid = jnp.stack(valid_parts, axis=0)
    context = (
        own_cols,
        own_global,
        send_list,
        send_valid,
        columns,
        grid_pos,
        grid_size,
        panel_len,
        distances,
    )
    current = blocks
    for turn in range(STEPS):
        square = pattern_product(current, current, context).astype(jnp.bfloat16)
        cube = pattern_product(current, square, context)
        current = (1.5 * current.astype(jnp.float32) - 0.5 * cube).astype(jnp.bfloat16)
    return current


def solution(mesh):
    placed = (P(("groups", "grid", "layer"), None, None, None), P("groups", None))
    return jax.shard_map(
        local,
        mesh=mesh,
        in_specs=placed,
        out_specs=P(("groups", "grid", "layer"), None, None, None),
        check_vma=False,
    )
```

profile of v0, /device:TPU:0, one launch (start us, length us, event | category | flops | bytes accessed | tf_op | source)
XLA Modules:
  0.0 231.5 jit_solution(15949181573232202069)
XLA Ops:
  6.5 0.7 all-gather.5.cloned.1.call-update
  7.3 0.9 constant_dynamic-slice_fusion.2
  8.2 0.7 convert_reduce_fusion.1
  9.1 0.6 convert_reduce_fusion
  9.9 1.0 sort.31
  10.9 1.0 sort.32
  11.8 0.6 gather_fusion
  12.5 0.6 compare_select_fusion.6
  13.1 5.1 %collective-permute-start = (s32[4]{0:T(128)S(1)}, s32[4]{0:T(128)S(1)}, u32[]{:S(2)}, u32[]{:S(2)}) collective-permute-start(s32[4]{0:T(128)S(1)} %compare_select_fusion.6), channel_id=1, source_target_pairs={{4,0},{8,4},{12,8},{0,12},{5,1},{9,5},{13,9},{1,13},{6,2},{10,6},{... | collective-permute-start | bytes 56 | tf_op jit(solution)/shard_map/ppermute | solution.py:12
  18.2 0.6 gather_fusion.1
  18.9 0.7 compare_select_fusion.4
  19.6 0.6 iota_compare_fusion.2
  20.3 0.7 iota_compare_fusion.1
  20.9 0.8 copy.104
  21.7 1.2 copy.109
  23.2 0.6 bitcast_select_fusion
  23.8 0.6 bitcast_select_fusion.1
  24.6 0.3 collective-permute-done.1
  25.0 0.6 gather_fusion.2
  25.6 2.8 %all-gather.5.cloned.1.call-done = bf16[8,4,128,128]{3,2,1,0:T(8,128)(2,1)} async-done(((bf16[2,4,128,128]{3,2,1,0:T(8,128)(2,1)}), bf16[8,4,128,128]{3,2,1,0:T(8,128)(2,1)}) %all-gather.5.cloned.1.call-update) | async-done | bytes 1048592 | tf_op jit(solution)/shard_map/all_gather | solution.py:32
  28.4 2.0 convolution_convert_fusion.3
  30.3 0.3 fusion.107
  30.7 3.4 %collective-permute-start.2 = (bf16[4,4,128,128]{3,0,2,1:T(4,128)(2,1)S(1)}, bf16[4,4,128,128]{3,0,2,1:T(4,128)(2,1)S(1)}, u32[]{:S(2)}, u32[]{:S(2)}) collective-permute-start(bf16[4,4,128,128]{3,0,2,1:T(4,128)(2,1)S(1)} %get-tuple-element.18), channel_id=1, source_target_pairs={{4,0},{8,4},{12,8},{0,12},{5,1},{9,5},{13,9},{1,13},{6,2},{10,6},{... | collective-permute-start | bytes 1572872 | tf_op jit(solution)/shard_map/ppermute | solution.py:12
  34.5 11.8 %collective-permute-done.2 = bf16[4,4,128,128]{3,0,2,1:T(4,128)(2,1)S(1)} collective-permute-done((bf16[4,4,128,128]{3,0,2,1:T(4,128)(2,1)S(1)}, bf16[4,4,128,128]{3,0,2,1:T(4,128)(2,1)S(1)}, u32[]{:S(2)}, u32[]{:S(2)}) %collective-permute-start.2) | collective-permute-done | bytes 524320 | tf_op jit(solution)/shard_map/ppermute | solution.py:12
  46.4 11.5 %collective-permute-done.3 = bf16[4,4,128,128]{3,0,2,1:T(4,128)(2,1)S(1)} collective-permute-done((bf16[4,4,128,128]{3,0,2,1:T(4,128)(2,1)S(1)}, bf16[4,4,128,128]{3,0,2,1:T(4,128)(2,1)S(1)}, u32[]{:S(2)}, u32[]{:S(2)}) %collective-permute-start.3) | collective-permute-done | bytes 524320 | tf_op jit(solution)/shard_map/ppermute | solution.py:12
  57.9 1.4 fusion.33
  59.3 0.5 fusion.45
  59.8 2.0 copy.111
  61.8 3.4 %convolution_bitcast_fusion.3 = f32[2,4,128,128]{3,1,2,0:T(4,128)S(1)} fusion(f32[2,4,4,128,128]{4,2,1,3,0:T(4,128)} %copy.111, s32[2,4]{1,0:T(2,128)S(1)} %copy.101, s32[2,4,4]{2,1,0:T(4,128)S(1)} %bitcast.85), kind=kOutput, calls=%fused_computation.38 | convolution fusion | flops 25165952 | bytes 2621600 | tf_op jit(solution)/shard_map/qtus,qtuik->qsik/dot_general | solution.py:67
  65.2 0.8 fusion.53
  66.0 15.2 %all-gather.7.cloned.1.call-done = bf16[8,4,128,128]{3,2,1,0:T(8,128)(2,1)} async-done(((bf16[2,4,128,128]{3,2,1,0:T(8,128)(2,1)}), bf16[8,4,128,128]{3,2,1,0:T(8,128)(2,1)}) %all-gather.7.cloned.1.call-update) | async-done | bytes 1048592 | tf_op jit(solution)/shard_map/all_gather | solution.py:32
  81.3 2.0 convolution_convert_fusion.2
  83.3 0.3 fusion.106
  83.6 3.4 %collective-permute-start.4 = (bf16[4,4,128,128]{3,0,2,1:T(4,128)(2,1)S(1)}, bf16[4,4,128,128]{3,0,2,1:T(4,128)(2,1)S(1)}, u32[]{:S(2)}, u32[]{:S(2)}) collective-permute-start(bf16[4,4,128,128]{3,0,2,1:T(4,128)(2,1)S(1)} %get-tuple-element.16), channel_id=1, source_target_pairs={{4,0},{8,4},{12,8},{0,12},{5,1},{9,5},{13,9},{1,13},{6,2},{10,6},{... | collective-permute-start | bytes 1572872 | tf_op jit(solution)/shard_map/ppermute | solution.py:12
  87.0 0.3 copy.114
  87.3 12.0 %collective-permute-done.4 = bf16[4,4,128,128]{3,0,2,1:T(4,128)(2,1)S(1)} collective-permute-done((bf16[4,4,128,128]{3,0,2,1:T(4,128)(2,1)S(1)}, bf16[4,4,128,128]{3,0,2,1:T(4,128)(2,1)S(1)}, u32[]{:S(2)}, u32[]{:S(2)}) %collective-permute-start.4) | collective-permute-done | bytes 524320 | tf_op jit(solution)/shard_map/ppermute | solution.py:12
  99.3 11.5 %collective-permute-done.5 = bf16[4,4,128,128]{3,0,2,1:T(4,128)(2,1)S(1)} collective-permute-done((bf16[4,4,128,128]{3,0,2,1:T(4,128)(2,1)S(1)}, bf16[4,4,128,128]{3,0,2,1:T(4,128)(2,1)S(1)}, u32[]{:S(2)}, u32[]{:S(2)}) %collective-permute-start.5) | collective-permute-done | bytes 524320 | tf_op jit(solution)/shard_map/ppermute | solution.py:12
  110.8 1.4 fusion.30
  112.2 0.5 fusion.42
  112.7 2.0 copy.116
  114.7 3.4 %convolution_bitcast_fusion.2 = f32[2,4,128,128]{3,1,2,0:T(4,128)S(1)} fusion(f32[2,4,4,128,128]{4,2,1,3,0:T(4,128)} %copy.116, s32[2,4]{1,0:T(2,128)S(1)} %copy.101, s32[2,4,4]{2,1,0:T(4,128)S(1)} %bitcast.86), kind=kOutput, calls=%fused_computation.37 | convolution fusion | flops 25165952 | bytes 2621600 | tf_op jit(solution)/shard_map/qtus,qtuik->qsik/dot_general | solution.py:67
  118.1 0.8 fusion.52
  119.0 15.2 %all-gather.9.cloned.1.call-done = bf16[8,4,128,128]{3,2,1,0:T(8,128)(2,1)} async-done(((bf16[2,4,128,128]{3,2,1,0:T(8,128)(2,1)}), bf16[8,4,128,128]{3,2,1,0:T(8,128)(2,1)}) %all-gather.9.cloned.1.call-update) | async-done | bytes 1048592 | tf_op jit(solution)/shard_map/all_gather | solution.py:32
  134.2 2.0 convolution_convert_fusion.1
  136.2 0.3 fusion.105
  136.5 3.4 %collective-permute-start.6 = (bf16[4,4,128,128]{3,0,2,1:T(4,128)(2,1)S(1)}, bf16[4,4,128,128]{3,0,2,1:T(4,128)(2,1)S(1)}, u32[]{:S(2)}, u32[]{:S(2)}) collective-permute-start(bf16[4,4,128,128]{3,0,2,1:T(4,128)(2,1)S(1)} %get-tuple-element.14), channel_id=1, source_target_pairs={{4,0},{8,4},{12,8},{0,12},{5,1},{9,5},{13,9},{1,13},{6,2},{10,6},{... | collective-permute-start | bytes 1572872 | tf_op jit(solution)/shard_map/ppermute | solution.py:12
  140.2 12.0 %collective-permute-done.6 = bf16[4,4,128,128]{3,0,2,1:T(4,128)(2,1)S(1)} collective-permute-done((bf16[4,4,128,128]{3,0,2,1:T(4,128)(2,1)S(1)}, bf16[4,4,128,128]{3,0,2,1:T(4,128)(2,1)S(1)}, u32[]{:S(2)}, u32[]{:S(2)}) %collective-permute-start.6) | collective-permute-done | bytes 524320 | tf_op jit(solution)/shard_map/ppermute | solution.py:12
  152.2 11.5 %collective-permute-done.7 = bf16[4,4,128,128]{3,0,2,1:T(4,128)(2,1)S(1)} collective-permute-done((bf16[4,4,128,128]{3,0,2,1:T(4,128)(2,1)S(1)}, bf16[4,4,128,128]{3,0,2,1:T(4,128)(2,1)S(1)}, u32[]{:S(2)}, u32[]{:S(2)}) %collective-permute-start.7) | collective-permute-done | bytes 524320 | tf_op jit(solution)/shard_map/ppermute | solution.py:12
  163.7 1.4 fusion.27
  165.1 0.5 fusion.39
  165.6 2.0 copy.121
  167.6 3.4 %convolution_bitcast_fusion.1 = f32[2,4,128,128]{3,1,2,0:T(4,128)S(1)} fusion(f32[2,4,4,128,128]{4,2,1,3,0:T(4,128)} %copy.121, s32[2,4]{1,0:T(2,128)S(1)} %copy.101, s32[2,4,4]{2,1,0:T(4,128)S(1)} %bitcast.87), kind=kOutput, calls=%fused_computation.36 | convolution fusion | flops 25165952 | bytes 2621600 | tf_op jit(solution)/shard_map/qtus,qtuik->qsik/dot_general | solution.py:67
  171.0 0.8 fusion.50
  171.9 15.3 %all-gather.11.cloned.1.call-done = bf16[8,4,128,128]{3,2,1,0:T(8,128)(2,1)} async-done(((bf16[2,4,128,128]{3,2,1,0:T(8,128)(2,1)}), bf16[8,4,128,128]{3,2,1,0:T(8,128)(2,1)}) %all-gather.11.cloned.1.call-update) | async-done | bytes 1048592 | tf_op jit(solution)/shard_map/all_gather | solution.py:32
  187.1 2.0 convolution_convert_fusion
  189.1 0.3 fusion.104
  189.5 3.4 %collective-permute-start.8 = (bf16[4,4,128,128]{3,0,2,1:T(4,128)(2,1)S(1)}, bf16[4,4,128,128]{3,0,2,1:T(4,128)(2,1)S(1)}, u32[]{:S(2)}, u32[]{:S(2)}) collective-permute-start(bf16[4,4,128,128]{3,0,2,1:T(4,128)(2,1)S(1)} %get-tuple-element.12), channel_id=1, source_target_pairs={{4,0},{8,4},{12,8},{0,12},{5,1},{9,5},{13,9},{1,13},{6,2},{10,6},{... | collective-permute-start | bytes 1572872 | tf_op jit(solution)/shard_map/ppermute | solution.py:12
  193.1 12.0 %collective-permute-done.8 = bf16[4,4,128,128]{3,0,2,1:T(4,128)(2,1)S(1)} collective-permute-done((bf16[4,4,128,128]{3,0,2,1:T(4,128)(2,1)S(1)}, bf16[4,4,128,128]{3,0,2,1:T(4,128)(2,1)S(1)}, u32[]{:S(2)}, u32[]{:S(2)}) %collective-permute-start.8) | collective-permute-done | bytes 524320 | tf_op jit(solution)/shard_map/ppermute | solution.py:12
  205.2 11.5 %collective-permute-done.9 = bf16[4,4,128,128]{3,0,2,1:T(4,128)(2,1)S(1)} collective-permute-done((bf16[4,4,128,128]{3,0,2,1:T(4,128)(2,1)S(1)}, bf16[4,4,128,128]{3,0,2,1:T(4,128)(2,1)S(1)}, u32[]{:S(2)}, u32[]{:S(2)}) %collective-permute-start.9) | collective-permute-done | bytes 524320 | tf_op jit(solution)/shard_map/ppermute | solution.py:12
  216.6 1.4 fusion.24
  218.0 1.9 fusion.36
  219.9 2.5 %copy.126 = f32[2,4,4,128,128]{4,2,1,3,0:T(4,128)S(1)} copy(f32[2,4,4,128,128]{3,4,2,1,0:T(8,128)} %bitcast.82) | data formatting | bytes 4194304 | tf_op jit(solution)/shard_map/reshape | solution.py:70
  222.4 1.8 convolution_bitcast_fusion
  224.2 0.8 fusion.49
  (51 shorter events, 2.2 us)
Async XLA Ops:
  6.5 21.8 %all-gather.5.cloned.1.call-start = ((), (), s32[]{:S(2)}) async-start(), calls=%async_computation | async-start | bytes 1310720 | tf_op jit(solution)/shard_map/all_gather | solution.py:32
  7.3 74.0 %all-gather.7.cloned.1.call-start = ((), (), s32[]{:S(2)}) async-start(), calls=%async_computation.1 | async-start | bytes 1310720 | tf_op jit(solution)/shard_map/all_gather | solution.py:32
  13.1 11.4 %collective-permute-start = (s32[4]{0:T(128)S(1)}, s32[4]{0:T(128)S(1)}, u32[]{:S(2)}, u32[]{:S(2)}) collective-permute-start(s32[4]{0:T(128)S(1)} %compare_select_fusion.6), channel_id=1, source_target_pairs={{4,0},{8,4},{12,8},{0,12},{5,1},{9,5},{13,9},{1,13},{6,2},{10,6},{... | collective-permute-start | bytes 56 | tf_op jit(solution)/shard_map/ppermute | solution.py:12
  19.5 5.4 %collective-permute-start.1 = (s32[4]{0:T(128)S(1)}, s32[4]{0:T(128)S(1)}, u32[]{:S(2)}, u32[]{:S(2)}) collective-permute-start(s32[4]{0:T(128)S(1)} %compare_select_fusion.4), channel_id=1, source_target_pairs={{12,0},{0,4},{4,8},{8,12},{13,1},{1,5},{5,9},{9,13},{14,2},{2,6},{... | collective-permute-start | bytes 56 | tf_op jit(solution)/shard_map/ppermute | solution.py:12
  30.7 15.7 %collective-permute-start.2 = (bf16[4,4,128,128]{3,0,2,1:T(4,128)(2,1)S(1)}, bf16[4,4,128,128]{3,0,2,1:T(4,128)(2,1)S(1)}, u32[]{:S(2)}, u32[]{:S(2)}) collective-permute-start(bf16[4,4,128,128]{3,0,2,1:T(4,128)(2,1)S(1)} %get-tuple-element.18), channel_id=1, source_target_pairs={{4,0},{8,4},{12,8},{0,12},{5,1},{9,5},{13,9},{1,13},{6,2},{10,6},{... | collective-permute-start | bytes 1572872 | tf_op jit(solution)/shard_map/ppermute | solution.py:12
  34.1 23.8 %collective-permute-start.3 = (bf16[4,4,128,128]{3,0,2,1:T(4,128)(2,1)S(1)}, bf16[4,4,128,128]{3,0,2,1:T(4,128)(2,1)S(1)}, u32[]{:S(2)}, u32[]{:S(2)}) collective-permute-start(bf16[4,4,128,128]{3,0,2,1:T(4,128)(2,1)S(1)} %get-tuple-element.19), channel_id=1, source_target_pairs={{12,0},{0,4},{4,8},{8,12},{13,1},{1,5},{5,9},{9,13},{14,2},{2,6},{... | collective-permute-start | bytes 1572872 | tf_op jit(solution)/shard_map/ppermute | solution.py:12
  34.5 24.7 %copy-start.1 = (bf16[2,4,128,128]{3,2,1,0:T(8,128)(2,1)S(1)}, bf16[2,4,128,128]{3,2,1,0:T(8,128)(2,1)}, u32[]{:S(2)}) copy-start(bf16[2,4,128,128]{3,2,1,0:T(8,128)(2,1)} %param.4) | copy-start | bytes 786436
  66.0 21.0 %copy-start.2 = (bf16[2,4,128,128]{3,2,1,0:T(8,128)(2,1)S(1)}, bf16[2,4,128,128]{3,2,1,0:T(8,128)(2,1)}, u32[]{:S(2)}) copy-start(bf16[2,4,128,128]{3,2,1,0:T(8,128)(2,1)} %fusion.53) | copy-start | bytes 786436
  66.0 68.2 %all-gather.9.cloned.1.call-start = ((), (), s32[]{:S(2)}) async-start(), calls=%async_computation.2 | async-start | bytes 1310720 | tf_op jit(solution)/shard_map/all_gather | solution.py:32
  83.6 15.7 %collective-permute-start.4 = (bf16[4,4,128,128]{3,0,2,1:T(4,128)(2,1)S(1)}, bf16[4,4,128,128]{3,0,2,1:T(4,128)(2,1)S(1)}, u32[]{:S(2)}, u32[]{:S(2)}) collective-permute-start(bf16[4,4,128,128]{3,0,2,1:T(4,128)(2,1)S(1)} %get-tuple-element.16), channel_id=1, source_target_pairs={{4,0},{8,4},{12,8},{0,12},{5,1},{9,5},{13,9},{1,13},{6,2},{10,6},{... | collective-permute-start | bytes 1572872 | tf_op jit(solution)/shard_map/ppermute | solution.py:12
  87.0 23.8 %collective-permute-start.5 = (bf16[4,4,128,128]{3,0,2,1:T(4,128)(2,1)S(1)}, bf16[4,4,128,128]{3,0,2,1:T(4,128)(2,1)S(1)}, u32[]{:S(2)}, u32[]{:S(2)}) collective-permute-start(bf16[4,4,128,128]{3,0,2,1:T(4,128)(2,1)S(1)} %get-tuple-element.17), channel_id=1, source_target_pairs={{12,0},{0,4},{4,8},{8,12},{13,1},{1,5},{5,9},{9,13},{14,2},{2,6},{... | collective-permute-start | bytes 1572872 | tf_op jit(solution)/shard_map/ppermute | solution.py:12
  118.9 21.0 %copy-start = (bf16[2,4,128,128]{3,2,1,0:T(8,128)(2,1)S(1)}, bf16[2,4,128,128]{3,2,1,0:T(8,128)(2,1)}, u32[]{:S(2)}) copy-start(bf16[2,4,128,128]{3,2,1,0:T(8,128)(2,1)} %fusion.52) | copy-start | bytes 786436
  118.9 68.2 %all-gather.11.cloned.1.call-start = ((), (), s32[]{:S(2)}) async-start(), calls=%async_computation.3 | async-start | bytes 1310720 | tf_op jit(solution)/shard_map/all_gather | solution.py:32
  136.5 15.7 %collective-permute-start.6 = (bf16[4,4,128,128]{3,0,2,1:T(4,128)(2,1)S(1)}, bf16[4,4,128,128]{3,0,2,1:T(4,128)(2,1)S(1)}, u32[]{:S(2)}, u32[]{:S(2)}) collective-permute-start(bf16[4,4,128,128]{3,0,2,1:T(4,128)(2,1)S(1)} %get-tuple-element.14), channel_id=1, source_target_pairs={{4,0},{8,4},{12,8},{0,12},{5,1},{9,5},{13,9},{1,13},{6,2},{10,6},{... | collective-permute-start | bytes 1572872 | tf_op jit(solution)/shard_map/ppermute | solution.py:12
  139.9 23.8 %collective-permute-start.7 = (bf16[4,4,128,128]{3,0,2,1:T(4,128)(2,1)S(1)}, bf16[4,4,128,128]{3,0,2,1:T(4,128)(2,1)S(1)}, u32[]{:S(2)}, u32[]{:S(2)}) collective-permute-start(bf16[4,4,128,128]{3,0,2,1:T(4,128)(2,1)S(1)} %get-tuple-element.15), channel_id=1, source_target_pairs={{12,0},{0,4},{4,8},{8,12},{13,1},{1,5},{5,9},{9,13},{14,2},{2,6},{... | collective-permute-start | bytes 1572872 | tf_op jit(solution)/shard_map/ppermute | solution.py:12
  171.8 21.0 %copy-start.3 = (bf16[2,4,128,128]{3,2,1,0:T(8,128)(2,1)S(1)}, bf16[2,4,128,128]{3,2,1,0:T(8,128)(2,1)}, u32[]{:S(2)}) copy-start(bf16[2,4,128,128]{3,2,1,0:T(8,128)(2,1)} %fusion.50) | copy-start | bytes 786436
  189.5 15.7 %collective-permute-start.8 = (bf16[4,4,128,128]{3,0,2,1:T(4,128)(2,1)S(1)}, bf16[4,4,128,128]{3,0,2,1:T(4,128)(2,1)S(1)}, u32[]{:S(2)}, u32[]{:S(2)}) collective-permute-start(bf16[4,4,128,128]{3,0,2,1:T(4,128)(2,1)S(1)} %get-tuple-element.12), channel_id=1, source_target_pairs={{4,0},{8,4},{12,8},{0,12},{5,1},{9,5},{13,9},{1,13},{6,2},{10,6},{... | collective-permute-start | bytes 1572872 | tf_op jit(solution)/shard_map/ppermute | solution.py:12
  192.8 23.8 %collective-permute-start.9 = (bf16[4,4,128,128]{3,0,2,1:T(4,128)(2,1)S(1)}, bf16[4,4,128,128]{3,0,2,1:T(4,128)(2,1)S(1)}, u32[]{:S(2)}, u32[]{:S(2)}) collective-permute-start(bf16[4,4,128,128]{3,0,2,1:T(4,128)(2,1)S(1)} %get-tuple-element.13), channel_id=1, source_target_pairs={{12,0},{0,4},{4,8},{8,12},{13,1},{1,5},{5,9},{9,13},{14,2},{2,6},{... | collective-permute-start | bytes 1572872 | tf_op jit(solution)/shard_map/ppermute | solution.py:12
Sparse Core Ops, SparseCore 0:
  8.9 19.4 all-gather.4
  66.1 15.1 all-gather.6
  119.0 15.1 all-gather.8
  172.0 15.1 all-gather.10
where the time goes:
time: 232 us
  waiting for transfers between devices  144 us (62%)
  matrix products  28.7 us (12%)
  starting transfers between devices  18.8 us (8%)
  local copies, waits for them, and re-layouts  16.3 us (7%)
  between operations  13.4 us (6%)
  other arithmetic  10.7 us (5%)
    ppermute x10, waiting for transfers between devices, from_behind(): return lax.ppermute(block, axis, route)  94.3 us
    all_gather x4, waiting for transfers between devices, pattern_product(): piece = lax.all_gather(operand, 'layer', axis=0, tiled=True)  48.5 us
    ppermute x10, starting transfers between devices, from_behind(): return lax.ppermute(block, axis, route)  18.7 us
    dot_general x4, matrix products, pattern_product(): jnp.einsum('qtus,qtuik->qsik', agree, partial_value.reshape(rows_own, slo...  12.1 us
    reshape x4, local copies, waits for them, and re-layouts, pattern_product(): partial_value.reshape(rows_own, slots, slots, width, width)  8.53 us
    dot_general x4, matrix products, pattern_product(): jnp.einsum('rn,nuij->ruij', picker, piece, preferred_element_type=jnp.flo...  7.85 us
    dot_general x4, matrix products, pattern_product(): jnp.einsum('ac,cuij->auij', matches.astype(jnp.bfloat16), cand_blocks, pr...  5.45 us
  transfers between devices with their start and end apart: 14, of which 13 were waited for; matrix products, arithmetic and copies ran while one was open for 6% of the time, Pallas kernels for 0%

commit v1 on v0

--- a/solution.py
+++ b/solution.py
@@ -1,6 +1,10 @@
+import functools
+
 import jax
 import jax.numpy as jnp
 from jax import lax
+from jax.experimental import pallas as pl
+from jax.experimental.pallas import tpu as pltpu
 from jax.sharding import PartitionSpec as P
 
 STEPS = 2
@@ -126,10 +130,315 @@
     return current
 
 
+GRID = 4
+LAYER = 4
+MESH = pl.DeviceIdType.MESH
+
+
+class Exchange:
+    def __init__(self, held, count, chunk, send, recv, place):
+        self.held, self.count, self.chunk = held, count, chunk
+        self.send, self.recv, self.place = send, recv, place
+        self.started = []
+
+    def part(self, side, layer, piece):
+        start = (side * LAYER + layer) * self.count + piece * self.chunk
+        return self.held.at[pl.ds(start, self.chunk)]
+
+    def copy(self, source, stage, side, layer, piece, target):
+        return pltpu.make_async_remote_copy(
+            src_ref=source,
+            dst_ref=self.part(side, layer, piece),
+            send_sem=self.send.at[stage, side, piece],
+            recv_sem=self.recv.at[stage, side, piece],
+            device_id=target,
+            device_id_type=MESH,
+        )
+
+    def start(self, source, stage, side, layer, piece, target):
+        copy = self.copy(source, stage, side, layer, piece, target)
+        copy.start()
+        self.started.append(copy)
+
+    def arrive(self, stage, side, layer, piece):
+        part = self.part(side, layer, piece)
+        self.copy(part, stage, side, layer, piece, {"layer": self.place.sibling}).wait_recv()
+
+    def pieces(self):
+        for piece in range(self.count // self.chunk):
+            for side in range(2):
+                yield side, piece
+
+    def begin(self, source):
+        at = self.place
+        for side, piece in self.pieces():
+            self.start(source(side, piece), 0, 1 - side, at.layer, piece, {"grid": at.panels[side]})
+
+    def spread(self):
+        at = self.place
+        for side, piece in self.pieces():
+            self.arrive(0, side, at.layer, piece)
+            part = self.part(side, at.layer, piece)
+            self.start(part, 2, side, at.layer, piece, {"layer": at.across})
+            self.start(part, 1, side, at.layer, piece, {"layer": at.sibling})
+
+    def relay(self):
+        at = self.place
+        for side, piece in self.pieces():
+            self.arrive(2, side, at.across, piece)
+            part = self.part(side, at.across, piece)
+            self.start(part, 3, side, at.across, piece, {"layer": at.sibling})
+
+    def finish(self):
+        at = self.place
+        for side, piece in self.pieces():
+            self.arrive(1, side, at.sibling, piece)
+            self.arrive(3, side, at.opposite, piece)
+
+    def drain(self):
+        for copy in self.started:
+            copy.wait_send()
+
+
+class Place:
+    def __init__(self):
+        self.grid = lax.axis_index("grid")
+        self.layer = lax.axis_index("layer")
+        self.panels = (
+            lax.rem(self.grid + 1, GRID),
+            lax.rem(self.grid + GRID - 1, GRID),
+        )
+        self.sibling = self.layer + 1 - 2 * lax.rem(self.layer, 2)
+        self.across = lax.rem(self.layer + 2, LAYER)
+        self.opposite = lax.rem(self.sibling + 2, LAYER)
+
+
+def dot(left, right):
+    return jnp.dot(left, right, preferred_element_type=jnp.float32)
+
+
+def kernel(
+    rows,
+    slots,
+    cap,
+    cols,
+    x,
+    out,
+    pack,
+    mutual,
+    diag,
+    sq_diag,
+    diag1,
+    sq_diag1,
+    own_sq,
+    own_diag1,
+    own_sq1,
+    sq,
+    sq_mut,
+    x1,
+    x1_mut,
+    send_m,
+    recv_m,
+    send_d,
+    recv_d,
+):
+    place = Place()
+    panel = rows * LAYER
+    first = (place.grid * LAYER + place.layer) * rows
+    width = x.shape[-1]
+    factor = (2.0 * width) ** (-0.5)
+    kept = [(a, t) for a in range(rows) for t in range(1, slots)]
+
+    barrier = pltpu.get_barrier_semaphore()
+    for target in (
+        {"grid": place.panels[0]},
+        {"grid": place.panels[1]},
+        {"layer": place.sibling},
+        {"layer": place.across},
+    ):
+        pl.semaphore_signal(barrier, inc=1, device_id=target, device_id_type=MESH)
+
+    own_cols = {(a, t): cols[first + a, t] for a, t in kept}
+    ahead = {
+        key: ((col // panel) == place.panels[0]).astype(jnp.int32) for key, col in own_cols.items()
+    }
+    for side in range(2):
+        source_row = [jnp.int32(0)] * cap
+        source_slot = [jnp.int32(1)] * cap
+        rank = jnp.int32(0)
+        for a, t in kept:
+            here = ahead[a, t] if side == 0 else 1 - ahead[a, t]
+            for k in range(cap):
+                taken = (here == 1) & (rank == k)
+                source_row[k] = jnp.where(taken, a, source_row[k])
+                source_slot[k] = jnp.where(taken, t, source_slot[k])
+            rank = rank + here
+        for k in range(cap):
+            pack[side, k] = x[source_row[k], source_slot[k]]
+    nothing = 2 * LAYER * cap
+    mutual[nothing] = jnp.zeros((width, width), jnp.bfloat16)
+
+    pl.semaphore_wait(barrier, 4)
+
+    def trade(held, which):
+        return Exchange(held, rows, 1, send_d.at[which], recv_d.at[which], place)
+
+    m_trade = Exchange(mutual, cap, MUTUAL_CHUNK, send_m, recv_m, place)
+    d_trade, s_trade, d1_trade, s1_trade = [
+        trade(held, which) for which, held in enumerate((diag, sq_diag, diag1, sq_diag1))
+    ]
+    m_trade.begin(lambda side, piece: pack.at[side, pl.ds(piece * MUTUAL_CHUNK, MUTUAL_CHUNK)])
+    d_trade.begin(lambda side, piece: x.at[piece, pl.ds(0, 1)])
+
+    at_diag = {}
+    at_mutual = {}
+    for a, t in kept:
+        col = own_cols[a, t]
+        side = 1 - ahead[a, t]
+        inner = lax.rem(col, panel)
+        owner = inner // rows
+        within = lax.rem(inner, rows)
+        start = col - within
+        at_diag[a, t] = (side * LAYER + owner) * rows + within
+        found = jnp.int32(nothing)
+        rank = jnp.int32(0)
+        for b, u in kept:
+            theirs = cols[start + b, u]
+            hit = (within == b) & (theirs == first + a)
+            found = jnp.where(hit, (side * LAYER + owner) * cap + rank, found)
+            rank = rank + (theirs // panel == place.grid).astype(jnp.int32)
+        at_mutual[a, t] = found
+
+    def row_dot(left, right):
+        return dot(jnp.concatenate(left, axis=1), jnp.concatenate(right, axis=0))
+
+    def rounded(product):
+        return (product * factor).astype(jnp.bfloat16)
+
+    def stepped(old, product):
+        return (1.5 * old.astype(jnp.float32) - 0.5 * (product * factor)).astype(jnp.bfloat16)
+
+    m_trade.spread()
+    d_trade.spread()
+    m_trade.relay()
+    m_trade.finish()
+
+    for a in range(rows):
+        met = [x[a, 0]] + [mutual[at_mutual[a, t]] for t in range(1, slots)]
+        own_sq[a] = rounded(row_dot([x[a, t] for t in range(slots)], met))
+    s_trade.begin(lambda side, piece: own_sq.at[pl.ds(piece, 1)])
+
+    d_trade.relay()
+    d_trade.finish()
+
+    for a, t in kept:
+        theirs, theirs_diag = mutual[at_mutual[a, t]], diag[at_diag[a, t]]
+        sq_mut[a, t - 1] = rounded(row_dot([theirs_diag, theirs], [theirs, x[a, 0]]))
+    for a in range(rows):
+        met = [own_sq[a]] + [sq_mut[a, t - 1] for t in range(1, slots)]
+        own_diag1[a] = stepped(x[a, 0], row_dot([x[a, t] for t in range(slots)], met))
+    d1_trade.begin(lambda side, piece: own_diag1.at[pl.ds(piece, 1)])
+
+    s_trade.spread()
+    for a, t in kept:
+        sq[a, t - 1] = rounded(row_dot([x[a, 0], x[a, t]], [x[a, t], diag[at_diag[a, t]]]))
+    s_trade.relay()
+    for a, t in kept:
+        theirs, theirs_diag = mutual[at_mutual[a, t]], diag[at_diag[a, t]]
+        x1_mut[a, t - 1] = stepped(
+            theirs, row_dot([theirs_diag, theirs], [sq_mut[a, t - 1], own_sq[a]])
+        )
+    s_trade.finish()
+
+    for a, t in kept:
+        x1[a, t - 1] = stepped(
+            x[a, t], row_dot([x[a, 0], x[a, t]], [sq[a, t - 1], sq_diag[at_diag[a, t]]])
+        )
+    for a in range(rows):
+        left = [own_diag1[a]] + [x1[a, t - 1] for t in range(1, slots)]
+        right = [own_diag1[a]] + [x1_mut[a, t - 1] for t in range(1, slots)]
+        own_sq1[a] = rounded(row_dot(left, right))
+    s1_trade.begin(lambda side, piece: own_sq1.at[pl.ds(piece, 1)])
+
+    d1_trade.spread()
+    d1_trade.relay()
+    d1_trade.finish()
+    s1_trade.spread()
+
+    for a, t in kept:
+        theirs, theirs_diag = x1_mut[a, t - 1], diag1[at_diag[a, t]]
+        sq_mut[a, t - 1] = rounded(row_dot([theirs_diag, theirs], [theirs, own_diag1[a]]))
+        sq[a, t - 1] = rounded(
+            row_dot([own_diag1[a], x1[a, t - 1]], [x1[a, t - 1], theirs_diag])
+        )
+    s1_trade.relay()
+    for a in range(rows):
+        left = [own_diag1[a]] + [x1[a, t - 1] for t in range(1, slots)]
+        met = [own_sq1[a]] + [sq_mut[a, t - 1] for t in range(1, slots)]
+        out[a, 0] = stepped(own_diag1[a], row_dot(left, met))
+    s1_trade.finish()
+    for a, t in kept:
+        out[a, t] = stepped(
+            x1[a, t - 1],
+            row_dot([own_diag1[a], x1[a, t - 1]], [sq[a, t - 1], sq_diag1[at_diag[a, t]]]),
+        )
+    for each in (m_trade, d_trade, s_trade, d1_trade, s1_trade):
+        each.drain()
+
+
+MUTUAL_CHUNK = 2
+
+
+def local_kernel(blocks, columns):
+    rows, slots, width, _ = blocks.shape
+    moved = rows * (slots - 1)
+    cap = 2 * ((moved + 3) // 4)
+
+    def held(*dims):
+        return pltpu.VMEM(dims + (width, width), jnp.bfloat16)
+
+    beside = 2 * LAYER * rows
+    m_sems = (4, 2, cap // MUTUAL_CHUNK)
+    d_sems = (4, 4, 2, rows)
+    return pl.pallas_call(
+        functools.partial(kernel, rows, slots, cap),
+        out_shape=jax.ShapeDtypeStruct(blocks.shape, blocks.dtype),
+        in_specs=[
+            pl.BlockSpec(memory_space=pltpu.SMEM),
+            pl.BlockSpec(memory_space=pltpu.VMEM),
+        ],
+        out_specs=pl.BlockSpec(memory_space=pltpu.VMEM),
+        scratch_shapes=[
+            held(2, cap),
+            held(2 * LAYER * cap + 1),
+            held(beside),
+            held(beside),
+            held(beside),
+            held(beside),
+            held(rows),
+            held(rows),
+            held(rows),
+            held(rows, slots - 1),
+            held(rows, slots - 1),
+            held(rows, slots - 1),
+            held(rows, slots - 1),
+            pltpu.SemaphoreType.DMA(m_sems),
+            pltpu.SemaphoreType.DMA(m_sems),
+            pltpu.SemaphoreType.DMA(d_sems),
+            pltpu.SemaphoreType.DMA(d_sems),
+        ],
+        compiler_params=pltpu.CompilerParams(
+            collective_id=0, has_side_effects=True, vmem_limit_bytes=32 * 1024 * 1024
+        ),
+        name="sign_iterations",
+    )(columns, blocks)
+
+
 def solution(mesh):
     placed = (P(("groups", "grid", "layer"), None, None, None), P("groups", None))
+    four_panels = mesh.shape["grid"] == GRID and mesh.shape["layer"] == LAYER
     return jax.shard_map(
-        local,
+        local_kernel if four_panels else local,
         mesh=mesh,
         in_specs=placed,
         out_specs=P(("groups", "grid", "layer"), None, None, None),

time: 232 us -> 45.8 us (0.20)
  waiting for transfers between devices: 144 us -> 0 us
  Pallas kernels: 0 us -> 43.2 us
  matrix products: 28.7 us -> 0 us
  starting transfers between devices: 18.8 us -> 0 us
  local copies, waits for them, and re-layouts: 16.3 us -> 2.42 us
  between operations: 13.4 us -> 0.01 us
  other arithmetic: 10.7 us -> 0 us
    ppermute x10 -> x0, waiting for transfers between devices: 94.3 us -> none  [from_behind(): return lax.ppermute(block, axis, route)]
    all_gather x4 -> x0, waiting for transfers between devices: 48.5 us -> none  [pattern_product(): piece = lax.all_gather(operand, 'layer', axis=0, tiled=True)]
    pallas_call x0 -> x1, Pallas kernels: none -> 43.2 us  [local_kernel(): pl.pallas_call(functools.partial(kernel, rows, slots, cap), out_shape=jax...]
    dot_general x16 -> x0, matrix products: 28.7 us -> none  [the longest x4 12.1 us: pattern_product(): jnp.einsum('qtus,qtuik->qsik', agree, partial_value.reshape(rows_own, slo...]
    ppermute x10 -> x0, starting transfers between devices: 18.7 us -> none  [from_behind(): return lax.ppermute(block, axis, route)]
    reshape x6 -> x0, local copies, waits for them, and re-layouts: 8.7 us -> none  [the longest x4 8.53 us: pattern_product(): partial_value.reshape(rows_own, slots, slots, width, width)]
    convert_element_type x4 -> x0, other arithmetic: 3.11 us -> none  [the longest x2 1.59 us: local(): (1.5 * current.astype(jnp.float32) - 0.5 * cube).astype(jnp.bfloat16)]
    select_n x7 -> x0, other arithmetic: 2.65 us -> none  [the longest x4 2.58 us: local(): list_parts.append(jnp.where(valid_now, local_rows, 0))]
  transfers between devices with their start and end apart: 14 -> 0, of which waited for: 13 -> 0; matrix products, arithmetic and copies ran while one was open for 6% -> 0% of each run, Pallas kernels for 0% -> 0%
where the time goes in v1:
time: 45.8 us; the launch traced here: 45.7 us
  Pallas kernels  43.2 us (94%)
  local copies, waits for them, and re-layouts  2.42 us (5%)
    pallas_call x1, Pallas kernels, local_kernel(): pl.pallas_call(functools.partial(kernel, rows, slots, cap), out_shape=jax...  43.2 us
    unnamed x4, local copies, waits for them, and re-layouts  2.42 us

profile of v1, /device:TPU:0, one launch (start us, length us, event | category | flops | bytes accessed | tf_op | source)
XLA Modules:
  0.0 45.7 jit_solution(7796312603899753374)
XLA Ops:
  0.0 0.8 %copy.3.cols = s32[32,4]{1,0:T(8,128)S(1)} copy(s32[32,4]{0,1:T(4,128)} %param.3) | data formatting | bytes 1024 | tf_op args[1]
  0.8 0.0 copy-start
  0.8 0.9 %copy-done = bf16[2,4,128,128]{3,2,1,0:T(8,128)(2,1)S(1)} copy-done((bf16[2,4,128,128]{3,2,1,0:T(8,128)(2,1)S(1)}, bf16[2,4,128,128]{3,2,1,0:T(8,128)(2,1)}, u32[]{:S(2)}) %copy-start) | copy-done | bytes 262168
  1.7 43.2 %sign_iterations.1 = bf16[2,4,128,128]{3,2,1,0:T(8,128)(2,1)S(1)} custom-call(s32[32,4]{1,0:T(8,128)S(1)} %copy.3.cols, bf16[2,4,128,128]{3,2,1,0:T(8,128)(2,1)S(1)} %copy-done), custom_call_target="tpu_custom_call" | custom-call | tf_op jit(solution)/shard_map/sign_iterations/pallas_call | solution.py:403
  45.0 0.7 %copy.5 = bf16[2,4,128,128]{3,2,1,0:T(8,128)(2,1)} copy(bf16[2,4,128,128]{3,2,1,0:T(8,128)(2,1)S(1)} %sign_iterations.1) | data formatting | bytes 524288
Async XLA Ops:
  0.8 0.9 %copy-start = (bf16[2,4,128,128]{3,2,1,0:T(8,128)(2,1)S(1)}, bf16[2,4,128,128]{3,2,1,0:T(8,128)(2,1)}, u32[]{:S(2)}) copy-start(bf16[2,4,128,128]{3,2,1,0:T(8,128)(2,1)} %x.1) | copy-start | bytes 786436

commit v2 on v1

--- a/solution.py
+++ b/solution.py
@@ -136,14 +136,12 @@
 
 
 class Exchange:
-    def __init__(self, held, count, chunk, send, recv, place):
-        self.held, self.count, self.chunk = held, count, chunk
-        self.send, self.recv, self.place = send, recv, place
+    def __init__(self, held, ways, send, recv, place):
+        self.held, self.ways, self.send, self.recv, self.place = held, ways, send, recv, place
         self.started = []
 
     def part(self, side, layer, piece):
-        start = (side * LAYER + layer) * self.count + piece * self.chunk
-        return self.held.at[pl.ds(start, self.chunk)]
+        return self.held.at[pl.ds((side * LAYER + layer) * len(self.ways) + piece, 1)]
 
     def copy(self, source, stage, side, layer, piece, target):
         return pltpu.make_async_remote_copy(
@@ -164,36 +162,45 @@
         part = self.part(side, layer, piece)
         self.copy(part, stage, side, layer, piece, {"layer": self.place.sibling}).wait_recv()
 
-    def pieces(self):
-        for piece in range(self.count // self.chunk):
-            for side in range(2):
-                yield side, piece
-
-    def begin(self, source):
+    def begin(self, source, pieces=None):
         at = self.place
-        for side, piece in self.pieces():
-            self.start(source(side, piece), 0, 1 - side, at.layer, piece, {"grid": at.panels[side]})
-
-    def spread(self):
+        for piece in range(len(self.ways)) if pieces is None else pieces:
+            for side in (at.far, 1 - at.far):
+                panel, mine = at.panel(side), source(side, piece)
+                self.start(mine, 0, 1 - side, at.layer, piece, {"grid": panel})
+                if self.ways[piece] == "direct":
+                    target = {"grid": panel, "layer": at.across}
+                    self.start(mine, 2, 1 - side, at.layer, piece, target)
+
+    def spread(self, pieces=None):
         at = self.place
-        for side, piece in self.pieces():
-            self.arrive(0, side, at.layer, piece)
-            part = self.part(side, at.layer, piece)
-            self.start(part, 2, side, at.layer, piece, {"layer": at.across})
-            self.start(part, 1, side, at.layer, piece, {"layer": at.sibling})
+        for piece in range(len(self.ways)) if pieces is None else pieces:
+            for side in (1 - at.far, at.far):
+                self.arrive(0, side, at.layer, piece)
+                part = self.part(side, at.layer, piece)
+                if self.ways[piece] != "direct":
+                    self.start(part, 2, side, at.layer, piece, {"layer": at.across})
+                if self.ways[piece] == "both":
+                    self.start(part, 3, side, at.layer, piece, {"layer": at.opposite})
+                self.start(part, 1, side, at.layer, piece, {"layer": at.sibling})
 
     def relay(self):
         at = self.place
-        for side, piece in self.pieces():
-            self.arrive(2, side, at.across, piece)
-            part = self.part(side, at.across, piece)
-            self.start(part, 3, side, at.across, piece, {"layer": at.sibling})
+        for piece, way in enumerate(self.ways):
+            for side in (1 - at.far, at.far):
+                if way != "both":
+                    self.arrive(2, side, at.across, piece)
+                    part = self.part(side, at.across, piece)
+                    self.start(part, 3, side, at.across, piece, {"layer": at.sibling})
 
     def finish(self):
         at = self.place
-        for side, piece in self.pieces():
-            self.arrive(1, side, at.sibling, piece)
-            self.arrive(3, side, at.opposite, piece)
+        for piece, way in enumerate(self.ways):
+            for side in (1 - at.far, at.far):
+                if way == "both":
+                    self.arrive(2, side, at.across, piece)
+                self.arrive(1, side, at.sibling, piece)
+                self.arrive(3, side, at.opposite, piece)
 
     def drain(self):
         for copy in self.started:
@@ -204,13 +211,25 @@
     def __init__(self):
         self.grid = lax.axis_index("grid")
         self.layer = lax.axis_index("layer")
-        self.panels = (
-            lax.rem(self.grid + 1, GRID),
-            lax.rem(self.grid + GRID - 1, GRID),
-        )
         self.sibling = self.layer + 1 - 2 * lax.rem(self.layer, 2)
         self.across = lax.rem(self.layer + 2, LAYER)
         self.opposite = lax.rem(self.sibling + 2, LAYER)
+        self.far = 1 - self.grid // (GRID - 1)
+
+    def panel(self, side):
+        return lax.rem(self.grid + 1 + (GRID - 2) * side, GRID)
+
+
+def calm(count):
+    return ["relay"] * count
+
+
+def urgent(count):
+    return ["both"] * (count - 1) + ["direct"]
+
+
+def mutual_ways(count):
+    return ["relay"] * (count - 2) + ["both", "direct"]
 
 
 def dot(left, right):
@@ -221,9 +240,11 @@
     rows,
     slots,
     cap,
+    cols_in,
+    x_in,
+    out,
     cols,
     x,
-    out,
     pack,
     mutual,
     diag,
@@ -241,6 +262,7 @@
     recv_m,
     send_d,
     recv_d,
+    load_sem,
 ):
     place = Place()
     panel = rows * LAYER
@@ -250,17 +272,24 @@
     kept = [(a, t) for a in range(rows) for t in range(1, slots)]
 
     barrier = pltpu.get_barrier_semaphore()
-    for target in (
-        {"grid": place.panels[0]},
-        {"grid": place.panels[1]},
-        {"layer": place.sibling},
-        {"layer": place.across},
-    ):
+    before, after = {"grid": place.panel(1)}, {"grid": place.panel(0)}
+    across = {"layer": place.across}
+    partners = [before, after, before | across, after | across, across]
+    partners += [{"layer": place.sibling}, {"layer": place.opposite}]
+    for target in partners:
         pl.semaphore_signal(barrier, inc=1, device_id=target, device_id_type=MESH)
-
-    own_cols = {(a, t): cols[first + a, t] for a, t in kept}
+    loads = [
+        pltpu.make_async_copy(cols_in, cols, load_sem.at[0]),
+        pltpu.make_async_copy(x_in, x, load_sem.at[1]),
+    ]
+    for load in loads:
+        load.start()
+    for load in loads:
+        load.wait()
+
+    own_cols = {(a, t): cols[t, first + a] for a, t in kept}
     ahead = {
-        key: ((col // panel) == place.panels[0]).astype(jnp.int32) for key, col in own_cols.items()
+        key: ((col // panel) == place.panel(0)).astype(jnp.int32) for key, col in own_cols.items()
     }
     for side in range(2):
         source_row = [jnp.int32(0)] * cap
@@ -278,16 +307,16 @@
     nothing = 2 * LAYER * cap
     mutual[nothing] = jnp.zeros((width, width), jnp.bfloat16)
 
-    pl.semaphore_wait(barrier, 4)
-
-    def trade(held, which):
-        return Exchange(held, rows, 1, send_d.at[which], recv_d.at[which], place)
-
-    m_trade = Exchange(mutual, cap, MUTUAL_CHUNK, send_m, recv_m, place)
+    pl.semaphore_wait(barrier, len(partners))
+
+    m_trade = Exchange(mutual, mutual_ways(cap), send_m, recv_m, place)
     d_trade, s_trade, d1_trade, s1_trade = [
-        trade(held, which) for which, held in enumerate((diag, sq_diag, diag1, sq_diag1))
+        Exchange(held, ways(rows), send_d.at[which], recv_d.at[which], place)
+        for which, (held, ways) in enumerate(
+            ((diag, calm), (sq_diag, urgent), (diag1, calm), (sq_diag1, urgent))
+        )
     ]
-    m_trade.begin(lambda side, piece: pack.at[side, pl.ds(piece * MUTUAL_CHUNK, MUTUAL_CHUNK)])
+    m_trade.begin(lambda side, piece: pack.at[side, pl.ds(piece, 1)])
     d_trade.begin(lambda side, piece: x.at[piece, pl.ds(0, 1)])
 
     at_diag = {}
@@ -303,7 +332,7 @@
         found = jnp.int32(nothing)
         rank = jnp.int32(0)
         for b, u in kept:
-            theirs = cols[start + b, u]
+            theirs = cols[u, start + b]
             hit = (within == b) & (theirs == first + a)
             found = jnp.where(hit, (side * LAYER + owner) * cap + rank, found)
             rank = rank + (theirs // panel == place.grid).astype(jnp.int32)
@@ -319,7 +348,6 @@
         return (1.5 * old.astype(jnp.float32) - 0.5 * (product * factor)).astype(jnp.bfloat16)
 
     m_trade.spread()
-    d_trade.spread()
     m_trade.relay()
     m_trade.finish()
 
@@ -328,8 +356,10 @@
         own_sq[a] = rounded(row_dot([x[a, t] for t in range(slots)], met))
     s_trade.begin(lambda side, piece: own_sq.at[pl.ds(piece, 1)])
 
+    d_trade.spread()
     d_trade.relay()
     d_trade.finish()
+    s_trade.spread([0])
 
     for a, t in kept:
         theirs, theirs_diag = mutual[at_mutual[a, t]], diag[at_diag[a, t]]
@@ -339,7 +369,7 @@
         own_diag1[a] = stepped(x[a, 0], row_dot([x[a, t] for t in range(slots)], met))
     d1_trade.begin(lambda side, piece: own_diag1.at[pl.ds(piece, 1)])
 
-    s_trade.spread()
+    s_trade.spread(range(1, rows))
     for a, t in kept:
         sq[a, t - 1] = rounded(row_dot([x[a, 0], x[a, t]], [x[a, t], diag[at_diag[a, t]]]))
     s_trade.relay()
@@ -361,9 +391,9 @@
     s1_trade.begin(lambda side, piece: own_sq1.at[pl.ds(piece, 1)])
 
     d1_trade.spread()
+    s1_trade.spread([0])
     d1_trade.relay()
     d1_trade.finish()
-    s1_trade.spread()
 
     for a, t in kept:
         theirs, theirs_diag = x1_mut[a, t - 1], diag1[at_diag[a, t]]
@@ -371,6 +401,7 @@
         sq[a, t - 1] = rounded(
             row_dot([own_diag1[a], x1[a, t - 1]], [x1[a, t - 1], theirs_diag])
         )
+    s1_trade.spread(range(1, rows))
     s1_trade.relay()
     for a in range(rows):
         left = [own_diag1[a]] + [x1[a, t - 1] for t in range(1, slots)]
@@ -386,9 +417,6 @@
         each.drain()
 
 
-MUTUAL_CHUNK = 2
-
-
 def local_kernel(blocks, columns):
     rows, slots, width, _ = blocks.shape
     moved = rows * (slots - 1)
@@ -398,17 +426,19 @@
         return pltpu.VMEM(dims + (width, width), jnp.bfloat16)
 
     beside = 2 * LAYER * rows
-    m_sems = (4, 2, cap // MUTUAL_CHUNK)
+    m_sems = (4, 2, cap)
     d_sems = (4, 4, 2, rows)
     return pl.pallas_call(
         functools.partial(kernel, rows, slots, cap),
         out_shape=jax.ShapeDtypeStruct(blocks.shape, blocks.dtype),
         in_specs=[
-            pl.BlockSpec(memory_space=pltpu.SMEM),
-            pl.BlockSpec(memory_space=pltpu.VMEM),
+            pl.BlockSpec(memory_space=pltpu.HBM),
+            pl.BlockSpec(memory_space=pltpu.HBM),
         ],
         out_specs=pl.BlockSpec(memory_space=pltpu.VMEM),
         scratch_shapes=[
+            pltpu.SMEM(columns.shape[::-1], columns.dtype),
+            pltpu.VMEM(blocks.shape, blocks.dtype),
             held(2, cap),
             held(2 * LAYER * cap + 1),
             held(beside),
@@ -426,12 +456,13 @@
             pltpu.SemaphoreType.DMA(m_sems),
             pltpu.SemaphoreType.DMA(d_sems),
             pltpu.SemaphoreType.DMA(d_sems),
+            pltpu.SemaphoreType.DMA((2,)),
         ],
         compiler_params=pltpu.CompilerParams(
-            collective_id=0, has_side_effects=True, vmem_limit_bytes=32 * 1024 * 1024
+            collective_id=0, has_side_effects=True, vmem_limit_bytes=64 * 1024 * 1024
         ),
         name="sign_iterations",
-    )(columns, blocks)
+    )(columns.T, blocks)
 
 
 def solution(mesh):

time: 45.8 us -> 41.1 us (0.90)
  Pallas kernels: 43.2 us -> 39.3 us
  local copies, waits for them, and re-layouts: 2.42 us -> 1.67 us
    pallas_call x1, Pallas kernels: 43.2 us -> 39.3 us  [local_kernel(): pl.pallas_call(functools.partial(kernel, rows, slots, cap), out_shape=jax...]
    unnamed x4 -> x1, local copies, waits for them, and re-layouts: 2.42 us -> 1.67 us
where the time goes in v2:
time: 41.1 us; the launch traced here: 41 us
  Pallas kernels  39.3 us (96%)
  local copies, waits for them, and re-layouts  1.67 us (4%)
    pallas_call x1, Pallas kernels, local_kernel(): pl.pallas_call(functools.partial(kernel, rows, slots, cap), out_shape=jax...  39.3 us
    unnamed x1, local copies, waits for them, and re-layouts  1.67 us

profile of v2, /device:TPU:0, one launch (start us, length us, event | category | flops | bytes accessed | tf_op | source)
XLA Modules:
  0.0 41.0 jit_solution(4476888489580603819)
XLA Ops:
  0.0 39.3 %sign_iterations.1 = bf16[2,4,128,128]{3,2,1,0:T(8,128)(2,1)} custom-call(s32[4,32]{1,0:T(4,128)} %bitcast.1, bf16[2,4,128,128]{3,2,1,0:T(8,128)(2,1)} %x_in.1), custom_call_target="tpu_custom_call" | custom-call | tf_op jit(solution)/shard_map/sign_iterations/pallas_call | solution.py:431
  39.3 1.7 %copy.4 = bf16[2,4,128,128]{3,2,1,0:T(8,128)(2,1)} copy(bf16[2,4,128,128]{3,2,1,0:T(8,128)(2,1)} %sign_iterations.1) | data formatting | bytes 524288

commit v3 on v2

--- a/solution.py
+++ b/solution.py
@@ -137,11 +137,15 @@
 
 class Exchange:
     def __init__(self, held, ways, send, recv, place):
-        self.held, self.ways, self.send, self.recv, self.place = held, ways, send, recv, place
+        self.held, self.send, self.recv, self.place = held, send, recv, place
+        self.ways = [way for way, _ in ways]
+        self.sizes = [size for _, size in ways]
+        self.starts = [sum(self.sizes[:piece]) for piece in range(len(ways))]
         self.started = []
 
     def part(self, side, layer, piece):
-        return self.held.at[pl.ds((side * LAYER + layer) * len(self.ways) + piece, 1)]
+        start = (side * LAYER + layer) * sum(self.sizes) + self.starts[piece]
+        return self.held.at[pl.ds(start, self.sizes[piece])]
 
     def copy(self, source, stage, side, layer, piece, target):
         return pltpu.make_async_remote_copy(
@@ -165,8 +169,9 @@
     def begin(self, source, pieces=None):
         at = self.place
         for piece in range(len(self.ways)) if pieces is None else pieces:
-            for side in (at.far, 1 - at.far):
-                panel, mine = at.panel(side), source(side, piece)
+            for side in (1 - at.far, at.far):
+                panel = at.panel(side)
+                mine = source(side, pl.ds(self.starts[piece], self.sizes[piece]))
                 self.start(mine, 0, 1 - side, at.layer, piece, {"grid": panel})
                 if self.ways[piece] == "direct":
                     target = {"grid": panel, "layer": at.across}
@@ -221,15 +226,15 @@
 
 
 def calm(count):
-    return ["relay"] * count
+    return [("relay", 1)] * count
 
 
 def urgent(count):
-    return ["both"] * (count - 1) + ["direct"]
+    return [("relay", 1)] * (count - 1) + [("direct", 1)]
 
 
 def mutual_ways(count):
-    return ["relay"] * (count - 2) + ["both", "direct"]
+    return [("relay", 1)] * (count - 1) + [("direct", 1)]
 
 
 def dot(left, right):
@@ -316,8 +321,8 @@
             ((diag, calm), (sq_diag, urgent), (diag1, calm), (sq_diag1, urgent))
         )
     ]
-    m_trade.begin(lambda side, piece: pack.at[side, pl.ds(piece, 1)])
-    d_trade.begin(lambda side, piece: x.at[piece, pl.ds(0, 1)])
+    m_trade.begin(lambda side, blocks: pack.at[side, blocks])
+    d_trade.begin(lambda side, blocks: x.at[blocks, 0])
 
     at_diag = {}
     at_mutual = {}
@@ -354,12 +359,13 @@
     for a in range(rows):
         met = [x[a, 0]] + [mutual[at_mutual[a, t]] for t in range(1, slots)]
         own_sq[a] = rounded(row_dot([x[a, t] for t in range(slots)], met))
-    s_trade.begin(lambda side, piece: own_sq.at[pl.ds(piece, 1)])
+    s_trade.begin(lambda side, blocks: own_sq.at[blocks])
 
     d_trade.spread()
+    m_trade.drain()
+    s_trade.spread([0])
     d_trade.relay()
     d_trade.finish()
-    s_trade.spread([0])
 
     for a, t in kept:
         theirs, theirs_diag = mutual[at_mutual[a, t]], diag[at_diag[a, t]]
@@ -367,9 +373,9 @@
     for a in range(rows):
         met = [own_sq[a]] + [sq_mut[a, t - 1] for t in range(1, slots)]
         own_diag1[a] = stepped(x[a, 0], row_dot([x[a, t] for t in range(slots)], met))
-    d1_trade.begin(lambda side, piece: own_diag1.at[pl.ds(piece, 1)])
-
-    s_trade.spread(range(1, rows))
+    d1_trade.begin(lambda side, blocks: own_diag1.at[blocks])
+
+    s_trade.spread(range(1, len(s_trade.ways)))
     for a, t in kept:
         sq[a, t - 1] = rounded(row_dot([x[a, 0], x[a, t]], [x[a, t], diag[at_diag[a, t]]]))
     s_trade.relay()
@@ -388,8 +394,10 @@
         left = [own_diag1[a]] + [x1[a, t - 1] for t in range(1, slots)]
         right = [own_diag1[a]] + [x1_mut[a, t - 1] for t in range(1, slots)]
         own_sq1[a] = rounded(row_dot(left, right))
-    s1_trade.begin(lambda side, piece: own_sq1.at[pl.ds(piece, 1)])
-
+    s1_trade.begin(lambda side, blocks: own_sq1.at[blocks])
+
+    d_trade.drain()
+    s_trade.drain()
     d1_trade.spread()
     s1_trade.spread([0])
     d1_trade.relay()
@@ -401,20 +409,20 @@
         sq[a, t - 1] = rounded(
             row_dot([own_diag1[a], x1[a, t - 1]], [x1[a, t - 1], theirs_diag])
         )
-    s1_trade.spread(range(1, rows))
+    s1_trade.spread(range(1, len(s1_trade.ways)))
     s1_trade.relay()
     for a in range(rows):
         left = [own_diag1[a]] + [x1[a, t - 1] for t in range(1, slots)]
         met = [own_sq1[a]] + [sq_mut[a, t - 1] for t in range(1, slots)]
         out[a, 0] = stepped(own_diag1[a], row_dot(left, met))
+    d1_trade.drain()
     s1_trade.finish()
     for a, t in kept:
         out[a, t] = stepped(
             x1[a, t - 1],
             row_dot([own_diag1[a], x1[a, t - 1]], [sq[a, t - 1], sq_diag1[at_diag[a, t]]]),
         )
-    for each in (m_trade, d_trade, s_trade, d1_trade, s1_trade):
-        each.drain()
+    s1_trade.drain()
 
 
 def local_kernel(blocks, columns):

time: 41.1 us -> 40.2 us (0.978)
  Pallas kernels: 39.3 us -> 38.2 us
    pallas_call x1, Pallas kernels: 39.3 us -> 38.2 us  [local_kernel(): pl.pallas_call(functools.partial(kernel, rows, slots, cap), out_shape=jax...]
where the time goes in v3:
time: 40.2 us; the launch traced here: 39.8 us
  Pallas kernels  38.2 us (95%)
  local copies, waits for them, and re-layouts  1.67 us (4%)
    pallas_call x1, Pallas kernels, local_kernel(): pl.pallas_call(functools.partial(kernel, rows, slots, cap), out_shape=jax...  38.2 us
    unnamed x1, local copies, waits for them, and re-layouts  1.67 us

profile of v3, /device:TPU:0, one launch (start us, length us, event | category | flops | bytes accessed | tf_op | source)
XLA Modules:
  0.0 39.8 jit_solution(6273218201193823989)
XLA Ops:
  0.0 38.2 %sign_iterations.1 = bf16[2,4,128,128]{3,2,1,0:T(8,128)(2,1)} custom-call(s32[4,32]{1,0:T(4,128)} %bitcast.1, bf16[2,4,128,128]{3,2,1,0:T(8,128)(2,1)} %x_in.1), custom_call_target="tpu_custom_call" | custom-call | tf_op jit(solution)/shard_map/sign_iterations/pallas_call | solution.py:439
  38.2 1.7 %copy.4 = bf16[2,4,128,128]{3,2,1,0:T(8,128)(2,1)} copy(bf16[2,4,128,128]{3,2,1,0:T(8,128)(2,1)} %sign_iterations.1) | data formatting | bytes 524288

commit v4 on v3

--- a/solution.py
+++ b/solution.py
@@ -189,9 +189,10 @@
                     self.start(part, 3, side, at.layer, piece, {"layer": at.opposite})
                 self.start(part, 1, side, at.layer, piece, {"layer": at.sibling})
 
-    def relay(self):
+    def relay(self, pieces=None):
         at = self.place
-        for piece, way in enumerate(self.ways):
+        for piece in range(len(self.ways)) if pieces is None else pieces:
+            way = self.ways[piece]
             for side in (1 - at.far, at.far):
                 if way != "both":
                     self.arrive(2, side, at.across, piece)
@@ -280,7 +281,7 @@
     before, after = {"grid": place.panel(1)}, {"grid": place.panel(0)}
     across = {"layer": place.across}
     partners = [before, after, before | across, after | across, across]
-    partners += [{"layer": place.sibling}, {"layer": place.opposite}]
+    partners += [{"layer": place.sibling}]
     for target in partners:
         pl.semaphore_signal(barrier, inc=1, device_id=target, device_id_type=MESH)
     loads = [
@@ -352,8 +353,10 @@
     def stepped(old, product):
         return (1.5 * old.astype(jnp.float32) - 0.5 * (product * factor)).astype(jnp.bfloat16)
 
-    m_trade.spread()
-    m_trade.relay()
+    m_trade.spread(range(cap - 1))
+    m_trade.relay([0])
+    m_trade.spread([cap - 1])
+    m_trade.relay(range(1, cap))
     m_trade.finish()
 
     for a in range(rows):

time: 40.2 us -> 40.2 us (level)
  no operation moved by 1% of the time
where the time goes in v4:
time: 40.2 us; the launch traced here: 39.8 us
  Pallas kernels  38.2 us (95%)
  local copies, waits for them, and re-layouts  1.67 us (4%)
    pallas_call x1, Pallas kernels, local_kernel(): pl.pallas_call(functools.partial(kernel, rows, slots, cap), out_shape=jax...  38.2 us
    unnamed x1, local copies, waits for them, and re-layouts  1.67 us

profile of v4, /device:TPU:0, one launch (start us, length us, event | category | flops | bytes accessed | tf_op | source)
XLA Modules:
  0.0 39.8 jit_solution(1306250173923426245)
XLA Ops:
  0.0 38.2 %sign_iterations.1 = bf16[2,4,128,128]{3,2,1,0:T(8,128)(2,1)} custom-call(s32[4,32]{1,0:T(4,128)} %bitcast.1, bf16[2,4,128,128]{3,2,1,0:T(8,128)(2,1)} %x_in.1), custom_call_target="tpu_custom_call" | custom-call | tf_op jit(solution)/shard_map/sign_iterations/pallas_call | solution.py:442
  38.2 1.7 %copy.4 = bf16[2,4,128,128]{3,2,1,0:T(8,128)(2,1)} copy(bf16[2,4,128,128]{3,2,1,0:T(8,128)(2,1)} %sign_iterations.1) | data formatting | bytes 524288
